TPU v7x, 32 devices: a whole 2x2x4 slice. The times are simulated.
32 devices in a mesh: grp: 2 (over x), chan: 16 (over z, y, core).
Axes of the slice: x: 2, y: 2, z: 4, core: 2. Of those that a mesh axis runs over, the one named last changes fastest.
Arguments:
- voltages: bfloat16 [4096, 64, 512], P('chan', 'grp'), parts along dimension 1, may hold values from -6 to 6
- exponents: int32 [64], P('grp'), parts along dimension 0, may hold values from 0 to 2, as said below
- pairs: int32 [128, 2], replicated, may hold values from 0 to 31, as said below
Outputs:
- visibilities: bfloat16 [64, 128, 2, 128, 128], P(('grp', 'chan')), parts along dimension 0
There are 2 independent parts, one for each index of `grp`. A program takes and returns all parts, laid end to end along the dimension named above; an argument that names none is the same for every part. Nothing has to cross between parts.
Inputs may be any that keep to these rules, and one draw needn't show every extreme that they name: exponents are whole numbers. The 128 pairs are distinct and each has first member at most its second.
All inputs are finite; a program needn't handle non-finite values.
Results may differ from a plain program's by a relative error of at most 0.001.
Values may be sent and summed in bfloat16 or wider, within the bound.
A program may use at most 192 MiB of HBM per device.

v0:
```python
import jax
import jax.numpy as jnp
from jax import lax
from jax.sharding import PartitionSpec as P

PANEL = 128
NT = 256


def correlate_plane(plane, pairs):
    width = plane.shape[1]
    half = width // 2
    count = plane.shape[0] // PANEL
    panels = plane.reshape(count, PANEL, width)
    group_size = 32
    groups = pairs.reshape(-1, group_size, 2)
    labels = jnp.arange(count, dtype=jnp.int32)

    def select(which):
        onehot = (which[:, None] == labels[None, :]).astype(jnp.bfloat16)
        picked = jnp.einsum("kn,nix->kix", onehot, panels, preferred_element_type=jnp.float32)
        return picked.astype(jnp.bfloat16).reshape(group_size, PANEL, 2, half)

    def one_group(chosen):
        left = select(chosen[:, 0])
        right = select(chosen[:, 1])
        quads = jnp.einsum("kiat,kjbt->kabij", left, right, preferred_element_type=jnp.float32)
        real_part = quads[:, 0, 0] + quads[:, 1, 1]
        imag_part = quads[:, 1, 0] - quads[:, 0, 1]
        return jnp.stack([real_part, imag_part], axis=1)

    return lax.map(one_group, groups).reshape(-1, 2, PANEL, PANEL)


def correlate_channels(turned, pairs):

    def one_channel(plane):
        return correlate_plane(plane, pairs)

    return lax.map(one_channel, jnp.moveaxis(turned, 1, 0))


def input_power(turned):
    wide = turned.astype(jnp.float32)
    return jnp.sum(wide * wide, axis=(1, 2))


def on_device(voltages, exponents, pairs):
    gain = jnp.exp2(-exponents.astype(jnp.float32)).astype(jnp.bfloat16)
    scaled = voltages * gain[None, :, None]
    total_samples = exponents.shape[0] * NT
    power = lax.all_gather(input_power(scaled), "chan", axis=0, tiled=True)
    turned = lax.all_to_all(scaled, "chan", split_axis=1, concat_axis=0, tiled=True)
    raw = correlate_channels(turned, pairs)
    mean_power = power / total_samples
    rows = mean_power.reshape(-1, PANEL)
    left_power = jnp.take(rows, pairs[:, 0], axis=0)
    right_power = jnp.take(rows, pairs[:, 1], axis=0)
    denom = jnp.sqrt(NT * left_power[:, :, None] * right_power[:, None, :])
    return (raw / denom[None, :, None, :, :]).astype(jnp.bfloat16)


def solution(mesh):
    return jax.shard_map(
        on_device,
        mesh=mesh,
        in_specs=(P("chan", "grp", None), P("grp"), P()),
        out_specs=P(("grp", "chan"), None, None, None, None),
        check_vma=False,
    )
```

profile of v0, /device:TPU:13, one launch (start us, length us, event | category | flops | bytes accessed | tf_op | source)
XLA Modules:
  0.0 682.7 jit_solution(13939410700513925443)
XLA Ops:
  0.7 9.6 %multiply_reduce_fusion = (f32[256]{0:T(256)S(1)}, bf16[256,32,512]{2,0,1:T(8,128)(2,1)}) fusion(bf16[32]{0:T(256)(128)(2,1)S(1)} %exponential_convert_fusion, bf16[256,32,512]{2,1,0:T(8,128)(2,1)} %param.9), kind=kLoop, calls=%fused_computation.29 | loop fusion | flops 16776960 | bytes 16778304 | tf_op jit(solution)/shard_map/reduce_sum | solution.py:45
  10.3 6.7 all-to-all-start
  17.0 191.7 %all-gather = f32[16,1,256]{2,1,0:T(1,128)S(1)} all-gather(f32[1,1,256]{2,1,0:T(1,128)S(1)} %bitcast.99), channel_id=1, replica_groups=mesh['grp'=2,'chan'=16] {'chan'}, dimensions={0}, use_global_device_ids=true | all-gather | bytes 17408 | tf_op jit(solution)/shard_map/all_gather | solution.py:52
  214.8 7.5 %copy.26 = bf16[16,256,2,512]{3,1,0,2:T(8,128)(2,1)} copy(bf16[16,256,2,512]{3,1,2,0:T(8,128)(2,1)} %bitcast.3) | data formatting | bytes 16777216 | tf_op jit(solution)/shard_map/all_to_all | solution.py:53
  222.2 440.5 %while.23 = (s32[]{:T(128)}, f32[2,128,2,128,128]{4,3,2,1,0:T(8,128)}, s32[128,2]{0,1:T(2,128)S(1)}, bf16[2,4096,512]{2,1,0:T(8,128)(2,1)}, s32[]{:T(128)}, /*index=5*/s32[]{:T(128)}, s32[]{:T(128)}) while((s32[]{:T(128)}, f32[2,128,2,128,128]{4,3,2,1,0:T(8,128)}, s32[128,2]{0,1:T(2,128)S(1)}, bf16[2,4096,512]{2,1,0:T(8,128)(2,1)}, s32[]{:T(128)}, ...), condition=%wide.region_3.4_spmd, body=%wide.region_0.3_spmd.sunk | while | flops 1348470784 | bytes 138415600 | solution.py:40
  229.2 201.7 %while.24 = (s32[]{:T(128)}, f32[4,32,2,128,128]{4,3,2,1,0:T(8,128)}, s32[4,32,2]{1,0,2:T(4,128)S(1)}, bf16[32,128,512]{2,0,1:T(8,128)(2,1)}, s32[]{:T(128)}) while((s32[]{:T(128)}, f32[4,32,2,128,128]{4,3,2,1,0:T(8,128)}, s32[4,32,2]{1,0,2:T(4,128)S(1)}, bf16[32,128,512]{2,0,1:T(8,128)(2,1)}, s32[]{:T(128)}) %tuple.52), condition=%wide.region_2.2_spmd.clone.clone, body=%wide.region_1.1_spmd.clone.clone.sunk | while | flops 1348470784 | bytes 88081744 | solution.py:32
  229.2 5.4 convolution_convert_fusion.4
  234.7 6.9 %reshape.106 = bf16[32,128,2,256]{3,2,0,1:T(2,128)(2,1)} reshape(bf16[32,128,512]{2,0,1:T(8,128)(2,1)} %convolution_convert_fusion.4) | data formatting | bytes 8388608 | tf_op jit(solution)/shard_map/while/body/eval_jaxpr/while/body/eval_jaxpr/reshape | solution.py:22
  241.6 5.4 convolution_convert_fusion.5
  247.0 6.9 %reshape.107 = bf16[32,128,2,256]{3,2,0,1:T(2,128)(2,1)} reshape(bf16[32,128,512]{2,0,1:T(8,128)(2,1)} %convolution_convert_fusion.5) | data formatting | bytes 8388608 | tf_op jit(solution)/shard_map/while/body/eval_jaxpr/while/body/eval_jaxpr/reshape | solution.py:22
  253.9 12.5 %fusion.36 = f32[32,2,2,128,128]{3,4,1,2,0:T(8,128)S(1)} fusion(bf16[32,128,2,256,1]{3,2,0,1,4:T(2,128)(2,1)} %bitcast.91, bf16[32,128,2,256,1]{3,2,0,1,4:T(2,128)(2,1)} %bitcast.92), kind=kOutput, calls=%fused_computation.7.clone.1 | convolution fusion | flops 1073741824 | bytes 16777216 | tf_op jit(solution)/shard_map/while/body/eval_jaxpr/while/body/eval_jaxpr/kiat,kjbt->kabij/dot_general | solution.py:27
  269.3 5.6 copy.55
  285.1 6.9 %reshape.106 = bf16[32,128,2,256]{3,2,0,1:T(2,128)(2,1)} reshape(bf16[32,128,512]{2,0,1:T(8,128)(2,1)} %convolution_convert_fusion.4) | data formatting | bytes 8388608 | tf_op jit(solution)/shard_map/while/body/eval_jaxpr/while/body/eval_jaxpr/reshape | solution.py:22
  292.0 5.4 convolution_convert_fusion.5
  297.4 6.9 %reshape.107 = bf16[32,128,2,256]{3,2,0,1:T(2,128)(2,1)} reshape(bf16[32,128,512]{2,0,1:T(8,128)(2,1)} %convolution_convert_fusion.5) | data formatting | bytes 8388608 | tf_op jit(solution)/shard_map/while/body/eval_jaxpr/while/body/eval_jaxpr/reshape | solution.py:22
  304.3 12.5 %fusion.36 = f32[32,2,2,128,128]{3,4,1,2,0:T(8,128)S(1)} fusion(bf16[32,128,2,256,1]{3,2,0,1,4:T(2,128)(2,1)} %bitcast.91, bf16[32,128,2,256,1]{3,2,0,1,4:T(2,128)(2,1)} %bitcast.92), kind=kOutput, calls=%fused_computation.7.clone.1 | convolution fusion | flops 1073741824 | bytes 16777216 | tf_op jit(solution)/shard_map/while/body/eval_jaxpr/while/body/eval_jaxpr/kiat,kjbt->kabij/dot_general | solution.py:27
  319.7 5.6 copy.55
  335.5 6.9 %reshape.106 = bf16[32,128,2,256]{3,2,0,1:T(2,128)(2,1)} reshape(bf16[32,128,512]{2,0,1:T(8,128)(2,1)} %convolution_convert_fusion.4) | data formatting | bytes 8388608 | tf_op jit(solution)/shard_map/while/body/eval_jaxpr/while/body/eval_jaxpr/reshape | solution.py:22
  342.4 5.4 convolution_convert_fusion.5
  347.9 6.9 %reshape.107 = bf16[32,128,2,256]{3,2,0,1:T(2,128)(2,1)} reshape(bf16[32,128,512]{2,0,1:T(8,128)(2,1)} %convolution_convert_fusion.5) | data formatting | bytes 8388608 | tf_op jit(solution)/shard_map/while/body/eval_jaxpr/while/body/eval_jaxpr/reshape | solution.py:22
  354.7 12.5 %fusion.36 = f32[32,2,2,128,128]{3,4,1,2,0:T(8,128)S(1)} fusion(bf16[32,128,2,256,1]{3,2,0,1,4:T(2,128)(2,1)} %bitcast.91, bf16[32,128,2,256,1]{3,2,0,1,4:T(2,128)(2,1)} %bitcast.92), kind=kOutput, calls=%fused_computation.7.clone.1 | convolution fusion | flops 1073741824 | bytes 16777216 | tf_op jit(solution)/shard_map/while/body/eval_jaxpr/while/body/eval_jaxpr/kiat,kjbt->kabij/dot_general | solution.py:27
  370.1 5.6 copy.55
  380.5 5.4 convolution_convert_fusion.4
  385.9 6.9 %reshape.106 = bf16[32,128,2,256]{3,2,0,1:T(2,128)(2,1)} reshape(bf16[32,128,512]{2,0,1:T(8,128)(2,1)} %convolution_convert_fusion.4) | data formatting | bytes 8388608 | tf_op jit(solution)/shard_map/while/body/eval_jaxpr/while/body/eval_jaxpr/reshape | solution.py:22
  392.8 5.4 convolution_convert_fusion.5
  398.3 6.9 %reshape.107 = bf16[32,128,2,256]{3,2,0,1:T(2,128)(2,1)} reshape(bf16[32,128,512]{2,0,1:T(8,128)(2,1)} %convolution_convert_fusion.5) | data formatting | bytes 8388608 | tf_op jit(solution)/shard_map/while/body/eval_jaxpr/while/body/eval_jaxpr/reshape | solution.py:22
  405.2 12.5 %fusion.36 = f32[32,2,2,128,128]{3,4,1,2,0:T(8,128)S(1)} fusion(bf16[32,128,2,256,1]{3,2,0,1,4:T(2,128)(2,1)} %bitcast.91, bf16[32,128,2,256,1]{3,2,0,1,4:T(2,128)(2,1)} %bitcast.92), kind=kOutput, calls=%fused_computation.7.clone.1 | convolution fusion | flops 1073741824 | bytes 16777216 | tf_op jit(solution)/shard_map/while/body/eval_jaxpr/while/body/eval_jaxpr/kiat,kjbt->kabij/dot_general | solution.py:27
  420.6 5.6 copy.55
  430.9 11.6 %bitcast_dynamic-update-slice_fusion.2 = f32[2,128,2,128,128]{4,3,2,1,0:T(8,128)} fusion(f32[2,128,2,128,128]{4,3,2,1,0:T(8,128)} %get-tuple-element.207, s32[]{:T(128)S(6)} %copy.66, f32[1,128,2,128,128]{4,3,2,1,0:T(8,128)} %bitcast.93), kind=kLoop, calls=%fused_computation.26.clone.1 | loop fusion | bytes 33554436 | tf_op jit(solution)/shard_map/while/body/jit(dynamic_update_index_in_dim)/dynamic_update_slice | solution.py:40
  449.5 201.6 %while.24 = (s32[]{:T(128)}, f32[4,32,2,128,128]{4,3,2,1,0:T(8,128)}, s32[4,32,2]{1,0,2:T(4,128)S(1)}, bf16[32,128,512]{2,0,1:T(8,128)(2,1)}, s32[]{:T(128)}) while((s32[]{:T(128)}, f32[4,32,2,128,128]{4,3,2,1,0:T(8,128)}, s32[4,32,2]{1,0,2:T(4,128)S(1)}, bf16[32,128,512]{2,0,1:T(8,128)(2,1)}, s32[]{:T(128)}) %tuple.52), condition=%wide.region_2.2_spmd.clone.clone, body=%wide.region_1.1_spmd.clone.clone.sunk | while | flops 1348470784 | bytes 88081744 | solution.py:32
  454.9 6.9 %reshape.106 = bf16[32,128,2,256]{3,2,0,1:T(2,128)(2,1)} reshape(bf16[32,128,512]{2,0,1:T(8,128)(2,1)} %convolution_convert_fusion.4) | data formatting | bytes 8388608 | tf_op jit(solution)/shard_map/while/body/eval_jaxpr/while/body/eval_jaxpr/reshape | solution.py:22
  467.3 6.9 %reshape.107 = bf16[32,128,2,256]{3,2,0,1:T(2,128)(2,1)} reshape(bf16[32,128,512]{2,0,1:T(8,128)(2,1)} %convolution_convert_fusion.5) | data formatting | bytes 8388608 | tf_op jit(solution)/shard_map/while/body/eval_jaxpr/while/body/eval_jaxpr/reshape | solution.py:22
  474.2 12.5 %fusion.36 = f32[32,2,2,128,128]{3,4,1,2,0:T(8,128)S(1)} fusion(bf16[32,128,2,256,1]{3,2,0,1,4:T(2,128)(2,1)} %bitcast.91, bf16[32,128,2,256,1]{3,2,0,1,4:T(2,128)(2,1)} %bitcast.92), kind=kOutput, calls=%fused_computation.7.clone.1 | convolution fusion | flops 1073741824 | bytes 16777216 | tf_op jit(solution)/shard_map/while/body/eval_jaxpr/while/body/eval_jaxpr/kiat,kjbt->kabij/dot_general | solution.py:27
  489.6 5.6 copy.55
  505.3 6.9 %reshape.106 = bf16[32,128,2,256]{3,2,0,1:T(2,128)(2,1)} reshape(bf16[32,128,512]{2,0,1:T(8,128)(2,1)} %convolution_convert_fusion.4) | data formatting | bytes 8388608 | tf_op jit(solution)/shard_map/while/body/eval_jaxpr/while/body/eval_jaxpr/reshape | solution.py:22
  517.7 6.9 %reshape.107 = bf16[32,128,2,256]{3,2,0,1:T(2,128)(2,1)} reshape(bf16[32,128,512]{2,0,1:T(8,128)(2,1)} %convolution_convert_fusion.5) | data formatting | bytes 8388608 | tf_op jit(solution)/shard_map/while/body/eval_jaxpr/while/body/eval_jaxpr/reshape | solution.py:22
  524.6 12.5 %fusion.36 = f32[32,2,2,128,128]{3,4,1,2,0:T(8,128)S(1)} fusion(bf16[32,128,2,256,1]{3,2,0,1,4:T(2,128)(2,1)} %bitcast.91, bf16[32,128,2,256,1]{3,2,0,1,4:T(2,128)(2,1)} %bitcast.92), kind=kOutput, calls=%fused_computation.7.clone.1 | convolution fusion | flops 1073741824 | bytes 16777216 | tf_op jit(solution)/shard_map/while/body/eval_jaxpr/while/body/eval_jaxpr/kiat,kjbt->kabij/dot_general | solution.py:27
  540.0 5.6 copy.55
  555.7 6.9 %reshape.106 = bf16[32,128,2,256]{3,2,0,1:T(2,128)(2,1)} reshape(bf16[32,128,512]{2,0,1:T(8,128)(2,1)} %convolution_convert_fusion.4) | data formatting | bytes 8388608 | tf_op jit(solution)/shard_map/while/body/eval_jaxpr/while/body/eval_jaxpr/reshape | solution.py:22
  568.1 6.9 %reshape.107 = bf16[32,128,2,256]{3,2,0,1:T(2,128)(2,1)} reshape(bf16[32,128,512]{2,0,1:T(8,128)(2,1)} %convolution_convert_fusion.5) | data formatting | bytes 8388608 | tf_op jit(solution)/shard_map/while/body/eval_jaxpr/while/body/eval_jaxpr/reshape | solution.py:22
  575.0 12.5 %fusion.36 = f32[32,2,2,128,128]{3,4,1,2,0:T(8,128)S(1)} fusion(bf16[32,128,2,256,1]{3,2,0,1,4:T(2,128)(2,1)} %bitcast.91, bf16[32,128,2,256,1]{3,2,0,1,4:T(2,128)(2,1)} %bitcast.92), kind=kOutput, calls=%fused_computation.7.clone.1 | convolution fusion | flops 1073741824 | bytes 16777216 | tf_op jit(solution)/shard_map/while/body/eval_jaxpr/while/body/eval_jaxpr/kiat,kjbt->kabij/dot_general | solution.py:27
  590.4 5.6 copy.55
  606.1 6.9 %reshape.106 = bf16[32,128,2,256]{3,2,0,1:T(2,128)(2,1)} reshape(bf16[32,128,512]{2,0,1:T(8,128)(2,1)} %convolution_convert_fusion.4) | data formatting | bytes 8388608 | tf_op jit(solution)/shard_map/while/body/eval_jaxpr/while/body/eval_jaxpr/reshape | solution.py:22
  618.5 6.9 %reshape.107 = bf16[32,128,2,256]{3,2,0,1:T(2,128)(2,1)} reshape(bf16[32,128,512]{2,0,1:T(8,128)(2,1)} %convolution_convert_fusion.5) | data formatting | bytes 8388608 | tf_op jit(solution)/shard_map/while/body/eval_jaxpr/while/body/eval_jaxpr/reshape | solution.py:22
  625.4 12.5 %fusion.36 = f32[32,2,2,128,128]{3,4,1,2,0:T(8,128)S(1)} fusion(bf16[32,128,2,256,1]{3,2,0,1,4:T(2,128)(2,1)} %bitcast.91, bf16[32,128,2,256,1]{3,2,0,1,4:T(2,128)(2,1)} %bitcast.92), kind=kOutput, calls=%fused_computation.7.clone.1 | convolution fusion | flops 1073741824 | bytes 16777216 | tf_op jit(solution)/shard_map/while/body/eval_jaxpr/while/body/eval_jaxpr/kiat,kjbt->kabij/dot_general | solution.py:27
  640.8 5.6 copy.55
  651.1 11.6 %bitcast_dynamic-update-slice_fusion.2 = f32[2,128,2,128,128]{4,3,2,1,0:T(8,128)} fusion(f32[2,128,2,128,128]{4,3,2,1,0:T(8,128)} %get-tuple-element.207, s32[]{:T(128)S(6)} %copy.66, f32[1,128,2,128,128]{4,3,2,1,0:T(8,128)} %bitcast.93), kind=kLoop, calls=%fused_computation.26.clone.1 | loop fusion | bytes 33554436 | tf_op jit(solution)/shard_map/while/body/jit(dynamic_update_index_in_dim)/dynamic_update_slice | solution.py:40
  662.7 19.9 %divide_convert_fusion = bf16[2,128,2,128,128]{4,3,2,1,0:T(8,128)(2,1)} fusion(f32[2,128,2,128,128]{4,3,2,1,0:T(8,128)} %get-tuple-element.58, f32[128,128,128]{2,1,0:T(8,128)} %multiply_sqrt_fusion), kind=kLoop, calls=%fused_computation.28 | loop fusion | flops 16777216 | bytes 58720256 | tf_op jit(solution)/shard_map/convert_element_type | solution.py:60
  (79 shorter events, 135.5 us)
Async XLA Ops:
  10.3 198.4 %copy-start = (s32[128,2]{0,1:T(2,128)S(1)}, s32[128,2]{0,1:T(2,128)}, u32[]{:S(2)}) copy-start(s32[128,2]{0,1:T(2,128)} %param.11) | copy-start | bytes 3076
  10.3 204.5 %all-to-all-start = ((bf16[256,32,512]{2,0,1:T(8,128)(2,1)}), bf16[256,32,512]{2,0,1:T(8,128)(2,1)}, u32[]{:S(2)}, u32[]{:S(2)}) async-start(bf16[256,32,512]{2,0,1:T(8,128)(2,1)} %get-tuple-element.112), calls=%async_computation | async-start | bytes 16777216 | tf_op jit(solution)/shard_map/all_to_all | solution.py:53
where the time goes:
time: 688 us; the launch traced here: 683 us
  local copies, waits for them, and re-layouts  239 us (35%)
  blocking collectives  192 us (28%)
  matrix products  187 us (27%)
  other arithmetic  57.9 us (8%)
    all_gather x1, blocking collectives, on_device(): power = lax.all_gather(input_power(scaled), 'chan', axis=0, tiled=True)  192 us
    reshape x16, local copies, waits for them, and re-layouts, select(): return picked.astype(jnp.bfloat16).reshape(group_size, PANEL, 2, half)  111 us
    dot_general x8, matrix products, one_group(): jnp.einsum('kiat,kjbt->kabij', left, right, preferred_element_type=jnp.fl...  100 us
    dot_general x16, matrix products, select(): jnp.einsum('kn,nix->kix', onehot, panels, preferred_element_type=jnp.floa...  86.8 us
    dynamic_update_slice x16, local copies, waits for them, and re-layouts, correlate_plane(): return lax.map(one_group, groups).reshape(-1, 2, PANEL, PANEL)  82.5 us
    dynamic_update_slice x2, local copies, waits for them, and re-layouts, correlate_channels(): return lax.map(one_channel, jnp.moveaxis(turned, 1, 0))  23.3 us
    convert_element_type x1, other arithmetic, on_device(): return (raw / denom[None, :, None, :, :]).astype(jnp.bfloat16)  19.9 us
    broadcast_in_dim x8, other arithmetic, correlate_plane(): return lax.map(one_group, groups).reshape(-1, 2, PANEL, PANEL)  18 us
  transfers between devices with their start and end apart: 1, of which 0 were waited for; matrix products, arithmetic and copies ran while one was open for 1% of the time, Pallas kernels for 0%

commit v1 on v0

v1 whole, which is shorter than its diff:
```python
import functools
import math

import jax
import jax.numpy as jnp
from jax import lax
from jax.experimental import pallas as pl
from jax.experimental.pallas import tpu as pltpu
from jax.sharding import PartitionSpec as P

PANEL = 128
NT = 256
GROUP = 16
VMEM_LIMIT = 56 * 1024 * 1024


def block_product(left, right, col, row):
    half = left.shape[1] // 2
    turned = jnp.concatenate([-right[:, half:], right[:, :half]], axis=1)
    both = jnp.concatenate([right, turned], axis=0)
    raw = lax.dot_general(left, both, (((1,), (1,)), ((), ())), preferred_element_type=jnp.float32)
    scale = col * row
    return (raw[:, :PANEL] * scale).astype(jnp.bfloat16), (raw[:, PANEL:] * scale).astype(jnp.bfloat16)


def turn_kernel(n, total, x_ref, pow_ref, pairs_ref, late_ref, vis_ref, col_ref, row_ref,
                early, stage, allpow, cols, rows, send, recv, psend, precv, local):
    me = lax.axis_index("chan")
    ants = early.shape[1]
    per = ants // PANEL

    barrier = pltpu.get_barrier_semaphore()

    @pl.loop(1, n)
    def _(off):
        pl.semaphore_signal(barrier, inc=1, device_id={"chan": lax.rem(me + off, n)},
                            device_id_type=pl.DeviceIdType.MESH)

    own_pow = pltpu.make_async_copy(pow_ref, allpow.at[me], local.at[0])
    own_early = pltpu.make_async_copy(x_ref.at[2 * me], early.at[me], local.at[1])
    own_late = pltpu.make_async_copy(x_ref.at[2 * me + 1], late_ref.at[me], local.at[2])
    own_pow.start()
    own_early.start()
    own_late.start()
    pl.semaphore_wait(barrier, n - 1)

    def pow_copy(off):
        return pltpu.make_async_remote_copy(
            src_ref=pow_ref, dst_ref=allpow.at[me], send_sem=psend.at[off], recv_sem=precv.at[off],
            device_id={"chan": lax.rem(me + off, n)}, device_id_type=pl.DeviceIdType.MESH)

    def data_copy(slot, off):
        dst = lax.rem(me + off, n)
        return pltpu.make_async_remote_copy(
            src_ref=x_ref.at[2 * dst + slot], dst_ref=(early, late_ref)[slot].at[me],
            send_sem=send.at[slot, off], recv_sem=recv.at[slot, off],
            device_id={"chan": dst}, device_id_type=pl.DeviceIdType.MESH)

    @pl.loop(1, n)
    def _(off):
        pow_copy(off).start()

    @pl.loop(1, n)
    def _(off):
        data_copy(0, off).start()

    @pl.loop(1, n)
    def _(off):
        data_copy(1, off).start()

    own_pow.wait()

    @pl.loop(1, n)
    def _(off):
        pow_copy(off).wait()

    for d in range(n):
        for h in range(per):
            p = d * per + h
            mean = allpow[d, 0:1, h * PANEL:(h + 1) * PANEL] / total
            rows[p] = jnp.broadcast_to(lax.rsqrt(mean), (8, PANEL))
            cols[p] = jnp.broadcast_to(lax.rsqrt(NT * mean), (PANEL, PANEL)).T
    col_out = pltpu.make_async_copy(cols, col_ref, local.at[3])
    row_out = pltpu.make_async_copy(rows, row_ref, local.at[4])
    col_out.start()
    row_out.start()

    own_early.wait()

    @pl.loop(1, n)
    def _(off):
        data_copy(0, off).wait()

    @pl.loop(0, pairs_ref.shape[0])
    def _(k):
        p, q = pairs_ref[k, 0], pairs_ref[k, 1]
        left = early[p // per, pl.ds(lax.rem(p, per) * PANEL, PANEL), :]
        right = early[q // per, pl.ds(lax.rem(q, per) * PANEL, PANEL), :]
        re, im = block_product(left, right, cols[p], rows[q, 0:1, :])
        stage[k, 0] = re
        stage[k, 1] = im

    vis_out = pltpu.make_async_copy(stage, vis_ref, local.at[5])
    vis_out.start()
    own_late.wait()

    @pl.loop(1, n)
    def _(off):
        data_copy(1, off).wait()

    vis_out.wait()
    col_out.wait()
    row_out.wait()


def finish_kernel(data_ref, vis_ref, cols, rows, pairs_ref, out_ref, stage, sems):
    nblk = pairs_ref.shape[0]
    groups = nblk // GROUP

    def old(g):
        part = pl.ds(g * GROUP, GROUP)
        return pltpu.make_async_copy(vis_ref.at[part], out_ref.at[0, part], sems.at[0, g])

    def new(g):
        part = pl.ds(g * GROUP, GROUP)
        return pltpu.make_async_copy(stage.at[part], out_ref.at[1, part], sems.at[1, g])

    for g in range(groups):
        old(g).start()

    for g in range(groups):
        @pl.loop(g * GROUP, (g + 1) * GROUP, unroll=4)
        def _(k):
            p, q = pairs_ref[k, 0], pairs_ref[k, 1]
            re, im = block_product(data_ref[p], data_ref[q], cols[p], rows[q, 0:1, :])
            stage[k, 0] = re
            stage[k, 1] = im
        new(g).start()

    for g in range(groups):
        old(g).wait()
        new(g).wait()


def on_device(n, voltages, exponents, pairs):
    ants, chans, width = voltages.shape
    assert chans == 2 * n and ants % PANEL == 0
    nblk = pairs.shape[0]
    panels = n * ants // PANEL
    gain = jnp.exp2(-exponents.astype(jnp.float32)).astype(jnp.bfloat16)
    scaled = voltages * gain[None, :, None]
    wide = scaled.astype(jnp.float32)
    power = jnp.sum(wide * wide, axis=(1, 2))
    power = jnp.broadcast_to(power[None, :], (8, ants))
    turned = jnp.swapaxes(scaled, 0, 1)

    hbm = pl.BlockSpec(memory_space=pl.ANY)
    vmem = pl.BlockSpec(memory_space=pltpu.VMEM)
    smem = pl.BlockSpec(memory_space=pltpu.SMEM)
    late, vis, cols, rows = pl.pallas_call(
        functools.partial(turn_kernel, n, float(chans * NT)),
        out_shape=[
            jax.ShapeDtypeStruct((n, ants, width), jnp.bfloat16),
            jax.ShapeDtypeStruct((nblk, 2, PANEL, PANEL), jnp.bfloat16),
            jax.ShapeDtypeStruct((panels, PANEL, PANEL), jnp.float32),
            jax.ShapeDtypeStruct((panels, 8, PANEL), jnp.float32),
        ],
        in_specs=[hbm, vmem, smem],
        out_specs=[hbm, hbm, hbm, hbm],
        scratch_shapes=[
            pltpu.VMEM((n, ants, width), jnp.bfloat16),
            pltpu.VMEM((nblk, 2, PANEL, PANEL), jnp.bfloat16),
            pltpu.VMEM((n, 8, ants), jnp.float32),
            pltpu.VMEM((panels, PANEL, PANEL), jnp.float32),
            pltpu.VMEM((panels, 8, PANEL), jnp.float32),
            pltpu.SemaphoreType.DMA((2, n)),
            pltpu.SemaphoreType.DMA((2, n)),
            pltpu.SemaphoreType.DMA((n,)),
            pltpu.SemaphoreType.DMA((n,)),
            pltpu.SemaphoreType.DMA((6,)),
        ],
        compiler_params=pltpu.CompilerParams(
            collective_id=0, has_side_effects=True, vmem_limit_bytes=VMEM_LIMIT),
        name="turn",
    )(turned, power, pairs)

    return pl.pallas_call(
        finish_kernel,
        out_shape=jax.ShapeDtypeStruct((2, nblk, 2, PANEL, PANEL), jnp.bfloat16),
        in_specs=[vmem, hbm, vmem, vmem, smem],
        out_specs=hbm,
        scratch_shapes=[
            pltpu.VMEM((nblk, 2, PANEL, PANEL), jnp.bfloat16),
            pltpu.SemaphoreType.DMA((2, nblk // GROUP)),
        ],
        compiler_params=pltpu.CompilerParams(vmem_limit_bytes=VMEM_LIMIT),
        name="finish",
    )(late.reshape(panels, PANEL, width), vis, cols, rows, pairs)


def solution(mesh):
    return jax.shard_map(
        functools.partial(on_device, mesh.shape["chan"]),
        mesh=mesh,
        in_specs=(P("chan", "grp", None), P("grp"), P()),
        out_specs=P(("grp", "chan"), None, None, None, None),
        check_vma=False,
    )
```

time: 688 us -> 475 us (0.69)
  Pallas kernels: 0 us -> 449 us
  local copies, waits for them, and re-layouts: 239 us -> 1.33 us
  blocking collectives: 192 us -> 0 us
  matrix products: 187 us -> 0 us
  other arithmetic: 57.9 us -> 24.6 us
    pallas_call x0 -> x2, Pallas kernels: none -> 449 us  [the longest x1 258 us: on_device(): pl.pallas_call(finish_kernel, out_shape=jax.ShapeDtypeStruct((2, nblk, 2,...]
    all_gather x1 -> x0, blocking collectives: 192 us -> none  [on_device(): power = lax.all_gather(input_power(scaled), 'chan', axis=0, tiled=True)]
    dot_general x24 -> x0, matrix products: 187 us -> none  [the longest x8 100 us: one_group(): jnp.einsum('kiat,kjbt->kabij', left, right, preferred_element_type=jnp.fl...]
    reshape x18 -> x0, local copies, waits for them, and re-layouts: 111 us -> none  [the longest x16 111 us: select(): return picked.astype(jnp.bfloat16).reshape(group_size, PANEL, 2, half)]
    dynamic_update_slice x18 -> x0, local copies, waits for them, and re-layouts: 106 us -> none  [the longest x16 82.5 us: correlate_plane(): return lax.map(one_group, groups).reshape(-1, 2, PANEL, PANEL)]
    convert_element_type x1 -> x0, other arithmetic: 19.9 us -> none  [on_device(): return (raw / denom[None, :, None, :, :]).astype(jnp.bfloat16)]
    broadcast_in_dim x9 -> x0, other arithmetic: 18 us -> none  [the longest x8 18 us: correlate_plane(): return lax.map(one_group, groups).reshape(-1, 2, PANEL, PANEL)]
    transpose x0 -> x1, other arithmetic: none -> 16.1 us  [on_device(): turned = jnp.swapaxes(scaled, 0, 1)]
  transfers between devices with their start and end apart: 1 -> 0, of which waited for: 0 -> 0; matrix products, arithmetic and copies ran while one was open for 1% -> 0% of each run, Pallas kernels for 0% -> 0%
where the time goes in v1:
time: 475 us
  Pallas kernels  449 us (95%)
  other arithmetic  24.6 us (5%)
    pallas_call x1, Pallas kernels, on_device(): pl.pallas_call(finish_kernel, out_shape=jax.ShapeDtypeStruct((2, nblk, 2,...  258 us
    pallas_call x1, Pallas kernels, on_device(): pl.pallas_call(functools.partial(turn_kernel, n, float(chans * NT)), out_...  191 us
    transpose x1, other arithmetic, on_device(): turned = jnp.swapaxes(scaled, 0, 1)  16.1 us

profile of v1, /device:TPU:13, one launch (start us, length us, event | category | flops | bytes accessed | tf_op | source)
XLA Modules:
  0.0 475.1 jit_solution(2612973553279003916)
XLA Ops:
  0.0 0.0 copy-start
  0.0 0.7 exponential_convert_fusion
  0.7 7.8 %multiply_reduce_fusion = f32[256]{0:T(256)S(1)} fusion(bf16[256,32,512]{2,1,0:T(8,128)(2,1)} %param.3, bf16[32]{0:T(256)(128)(2,1)S(1)} %exponential_convert_fusion), kind=kLoop, calls=%fused_computation | loop fusion | flops 16776960 | bytes 8389696 | tf_op jit(solution)/shard_map/reduce_sum | solution.py:153
  8.5 0.6 broadcast_in_dim.2.pow_ref
  9.1 0.0 copy-done
  9.1 0.7 copy.5.pairs_ref
  9.8 16.1 %fusion.x_ref = bf16[32,256,512]{2,1,0:T(8,128)(2,1)} fusion(bf16[256,32,512]{2,1,0:T(8,128)(2,1)} %param.3, bf16[32]{0:T(256)(128)(2,1)S(1)} %exponential_convert_fusion), kind=kLoop, calls=%fused_computation.2 | loop fusion | flops 4194304 | bytes 16777280 | tf_op jit(solution)/shard_map/transpose | solution.py:155
  26.0 190.8 %turn.1 = (bf16[16,256,512]{2,1,0:T(8,128)(2,1)}, bf16[128,2,128,128]{3,2,1,0:T(8,128)(2,1)}, f32[32,128,128]{2,1,0:T(8,128)}, f32[32,8,128]{2,1,0:T(8,128)}) custom-call(bf16[32,256,512]{2,1,0:T(8,128)(2,1)} %fusion.x_ref, f32[8,256]{1,0:T(8,128)} %broadcast_in_dim.2.pow_ref, s32[128,2]{1,0:T(8,128)} %copy.5.pairs_ref), custom_call_target="tpu_custom_call" | custom-call | tf_op jit(solution)/shard_map/turn/pallas_call | solution.py:160
  216.7 258.2 %finish.1 = bf16[2,128,2,128,128]{4,3,2,1,0:T(8,128)(2,1)} custom-call(bf16[32,128,512]{2,1,0:T(8,128)(2,1)} %bitcast.3, bf16[128,2,128,128]{3,2,1,0:T(8,128)(2,1)} %get-tuple-element.10.vis_ref, f32[32,128,128]{2,1,0:T(8,128)} %get-tuple-element.11.cols, f32[32,8,128]{2,1,0:T(8,128)} %get-tuple-element.12.rows, s32[128,2]{1,0:T(8,128)} %copy.5.pairs_ref), custom_call_target="tpu_custom_call" | custom-call | tf_op jit(solution)/shard_map/finish/pallas_call | solution.py:187
Async XLA Ops:
  0.0 9.1 %copy-start = (s32[128,2]{0,1:T(2,128)S(1)}, s32[128,2]{0,1:T(2,128)}, u32[]{:S(2)}) copy-start(s32[128,2]{0,1:T(2,128)} %param.5) | copy-start | bytes 3076

commit v2 on v1

v2 whole, which is shorter than its diff:
```python
import functools
import math

import jax
import jax.numpy as jnp
from jax import lax
from jax.experimental import pallas as pl
from jax.experimental.pallas import tpu as pltpu
from jax.sharding import PartitionSpec as P

PANEL = 128
NT = 256
GROUP = 16
VMEM_LIMIT = 56 * 1024 * 1024


def block_product(left, right, col, row):
    half = left.shape[1] // 2
    turned = jnp.concatenate([-right[:, half:], right[:, :half]], axis=1)
    both = jnp.concatenate([right, turned], axis=0)
    raw = lax.dot_general(left, both, (((1,), (1,)), ((), ())), preferred_element_type=jnp.float32)
    scale = col * row
    return (raw[:, :PANEL] * scale).astype(jnp.bfloat16), (raw[:, PANEL:] * scale).astype(jnp.bfloat16)


def turn_kernel(n, total, x_ref, exps_ref, pairs_ref, late_ref, vis_ref, col_ref, row_ref,
                raw, wide, outbox, early, stage, sums, ownpow, allpow, cols, rows,
                send, recv, lsend, lrecv, psend, precv, insem, local):
    me = lax.axis_index("chan")
    pieces, size, chans, width = raw.shape
    ants = pieces * size
    per = ants // PANEL
    lanes = width // 128

    def in_copy(b):
        return pltpu.make_async_copy(x_ref.at[pl.ds(b * size, size)], raw.at[b], insem.at[b])

    for b in range(pieces):
        in_copy(b).start()

    barrier = pltpu.get_barrier_semaphore()

    @pl.loop(1, n)
    def _(off):
        pl.semaphore_signal(barrier, inc=1, device_id={"chan": lax.rem(me + off, n)},
                            device_id_type=pl.DeviceIdType.MESH)

    def pow_copy(off):
        return pltpu.make_async_remote_copy(
            src_ref=ownpow, dst_ref=allpow.at[me], send_sem=psend.at[off], recv_sem=precv.at[off],
            device_id={"chan": lax.rem(me + off, n)}, device_id_type=pl.DeviceIdType.MESH)

    def early_copy(b, off):
        dst = lax.rem(me + off, n)
        part = pl.ds(b * size, size)
        return pltpu.make_async_remote_copy(
            src_ref=outbox.at[2 * dst, part], dst_ref=early.at[me, part],
            send_sem=send.at[b, off], recv_sem=recv.at[b, off],
            device_id={"chan": dst}, device_id_type=pl.DeviceIdType.MESH)

    def late_copy(off):
        dst = lax.rem(me + off, n)
        return pltpu.make_async_remote_copy(
            src_ref=outbox.at[2 * dst + 1], dst_ref=late_ref.at[me],
            send_sem=lsend.at[off], recv_sem=lrecv.at[off],
            device_id={"chan": dst}, device_id_type=pl.DeviceIdType.MESH)

    for b in range(pieces):
        in_copy(b).wait()

        @pl.loop(0, size // 2)
        def _(a):
            for i in range(2):
                row = raw[b, a * 2 + i].astype(jnp.float32)
                at = pl.ds(pl.multiple_of((a * 2 + i) * chans, chans), chans)
                for t in range(lanes):
                    wide[t, at, :] = row[:, t * 128:(t + 1) * 128]

        def channel(c, acc):
            gain = lax.shift_left(jnp.int32(1), 30 - exps_ref[c]).astype(jnp.float32) * 2.0 ** -30
            for t in range(lanes):
                v = wide[t, pl.ds(c, size, stride=chans), :] * gain
                acc = acc + v * v
                outbox[c, b * size:(b + 1) * size, t * 128:(t + 1) * 128] = v.astype(jnp.bfloat16)
            return acc

        acc = lax.fori_loop(0, chans, channel, jnp.zeros((size, 128), jnp.float32))
        sums[b * size:(b + 1) * size, :] = acc
        if b == 0:
            pl.semaphore_wait(barrier, n - 1)

        @pl.loop(1, n)
        def _(off):
            early_copy(b, off).start()

    for h in range(per):
        row = jnp.sum(sums[h * PANEL:(h + 1) * PANEL, :].T, axis=0, keepdims=True)
        ownpow[:, h * PANEL:(h + 1) * PANEL] = jnp.broadcast_to(row, (8, PANEL))

    @pl.loop(1, n)
    def _(off):
        pow_copy(off).start()

    @pl.loop(1, n)
    def _(off):
        late_copy(off).start()

    own_pow = pltpu.make_async_copy(ownpow, allpow.at[me], local.at[0])
    own_early = pltpu.make_async_copy(outbox.at[2 * me], early.at[me], local.at[1])
    own_late = pltpu.make_async_copy(outbox.at[2 * me + 1], late_ref.at[me], local.at[2])
    own_pow.start()
    own_early.start()
    own_late.start()
    own_pow.wait()

    @pl.loop(1, n)
    def _(off):
        pow_copy(off).wait()

    @pl.loop(0, n)
    def _(d):
        for h in range(per):
            p = d * per + h
            mean = allpow[d, 0:1, h * PANEL:(h + 1) * PANEL] / total
            rows[p] = jnp.broadcast_to(lax.rsqrt(mean), (8, PANEL))
            cols[p] = jnp.broadcast_to(lax.rsqrt(NT * mean), (PANEL, PANEL)).T

    col_out = pltpu.make_async_copy(cols, col_ref, local.at[3])
    row_out = pltpu.make_async_copy(rows, row_ref, local.at[4])
    col_out.start()
    row_out.start()
    own_early.wait()

    for b in range(pieces):
        @pl.loop(1, n)
        def _(off):
            early_copy(b, off).wait()

    @pl.loop(0, pairs_ref.shape[1])
    def _(k):
        p, q = pairs_ref[0, k], pairs_ref[1, k]
        left = early[p // per, pl.ds(lax.rem(p, per) * PANEL, PANEL), :]
        right = early[q // per, pl.ds(lax.rem(q, per) * PANEL, PANEL), :]
        re, im = block_product(left, right, cols[p], rows[q, 0:1, :])
        stage[k, 0] = re
        stage[k, 1] = im

    vis_out = pltpu.make_async_copy(stage, vis_ref, local.at[5])
    vis_out.start()
    own_late.wait()

    @pl.loop(1, n)
    def _(off):
        late_copy(off).wait()

    vis_out.wait()
    col_out.wait()
    row_out.wait()


def finish_kernel(data_ref, vis_ref, col_ref, rows, pairs_ref, out_ref, data, cols, first, stage, insem, sems):
    nblk = pairs_ref.shape[1]
    groups = nblk // GROUP

    data_in = pltpu.make_async_copy(data_ref, data, insem.at[groups])
    cols_in = pltpu.make_async_copy(col_ref, cols, insem.at[groups + 1])
    data_in.start()
    cols_in.start()

    def fetch(g):
        part = pl.ds(g * GROUP, GROUP)
        return pltpu.make_async_copy(vis_ref.at[part], first.at[part], insem.at[g])

    def old(g):
        part = pl.ds(g * GROUP, GROUP)
        return pltpu.make_async_copy(first.at[part], out_ref.at[0, part], sems.at[0, g])

    def new(g):
        part = pl.ds(g * GROUP, GROUP)
        return pltpu.make_async_copy(stage.at[part], out_ref.at[1, part], sems.at[1, g])

    for g in range(groups):
        fetch(g).start()
    data_in.wait()
    cols_in.wait()

    for g in range(groups):
        @pl.loop(g * GROUP, (g + 1) * GROUP, unroll=4)
        def _(k):
            p, q = pairs_ref[0, k], pairs_ref[1, k]
            re, im = block_product(data[p], data[q], cols[p], rows[q, 0:1, :])
            stage[k, 0] = re
            stage[k, 1] = im
        new(g).start()
        fetch(g).wait()
        old(g).start()

    for g in range(groups):
        old(g).wait()
        new(g).wait()


def on_device(n, voltages, exponents, pairs):
    ants, chans, width = voltages.shape
    assert chans == 2 * n and ants % PANEL == 0
    nblk = pairs.shape[0]
    panels = n * ants // PANEL
    size = 64
    pieces = ants // size
    pairs = pairs.T

    hbm = pl.BlockSpec(memory_space=pl.ANY)
    vmem = pl.BlockSpec(memory_space=pltpu.VMEM)
    smem = pl.BlockSpec(memory_space=pltpu.SMEM)
    dma = pltpu.SemaphoreType.DMA
    late, vis, cols, rows = pl.pallas_call(
        functools.partial(turn_kernel, n, float(chans * NT)),
        out_shape=[
            jax.ShapeDtypeStruct((n, ants, width), jnp.bfloat16),
            jax.ShapeDtypeStruct((nblk, 2, PANEL, PANEL), jnp.bfloat16),
            jax.ShapeDtypeStruct((panels, PANEL, PANEL), jnp.float32),
            jax.ShapeDtypeStruct((panels, 8, PANEL), jnp.float32),
        ],
        in_specs=[hbm, smem, smem],
        out_specs=[hbm, hbm, hbm, hbm],
        scratch_shapes=[
            pltpu.VMEM((pieces, size, chans, width), jnp.bfloat16),
            pltpu.VMEM((width // 128, size * chans, 128), jnp.float32),
            pltpu.VMEM((chans, ants, width), jnp.bfloat16),
            pltpu.VMEM((n, ants, width), jnp.bfloat16),
            pltpu.VMEM((nblk, 2, PANEL, PANEL), jnp.bfloat16),
            pltpu.VMEM((ants, 128), jnp.float32),
            pltpu.VMEM((8, ants), jnp.float32),
            pltpu.VMEM((n, 8, ants), jnp.float32),
            pltpu.VMEM((panels, PANEL, PANEL), jnp.float32),
            pltpu.VMEM((panels, 8, PANEL), jnp.float32),
            dma((pieces, n)), dma((pieces, n)), dma((n,)), dma((n,)), dma((n,)), dma((n,)),
            dma((pieces,)), dma((6,)),
        ],
        compiler_params=pltpu.CompilerParams(
            collective_id=0, has_side_effects=True, vmem_limit_bytes=VMEM_LIMIT),
        name="turn",
    )(voltages, exponents, pairs)

    return pl.pallas_call(
        finish_kernel,
        out_shape=jax.ShapeDtypeStruct((2, nblk, 2, PANEL, PANEL), jnp.bfloat16),
        in_specs=[hbm, hbm, hbm, vmem, smem],
        out_specs=hbm,
        scratch_shapes=[
            pltpu.VMEM((panels, PANEL, width), jnp.bfloat16),
            pltpu.VMEM((panels, PANEL, PANEL), jnp.float32),
            pltpu.VMEM((nblk, 2, PANEL, PANEL), jnp.bfloat16),
            pltpu.VMEM((nblk, 2, PANEL, PANEL), jnp.bfloat16),
            dma((nblk // GROUP + 2,)),
            dma((2, nblk // GROUP)),
        ],
        compiler_params=pltpu.CompilerParams(vmem_limit_bytes=VMEM_LIMIT),
        name="finish",
    )(late.reshape(panels, PANEL, width), vis, cols, rows, pairs)


def solution(mesh):
    return jax.shard_map(
        functools.partial(on_device, mesh.shape["chan"]),
        mesh=mesh,
        in_specs=(P("chan", "grp", None), P("grp"), P()),
        out_specs=P(("grp", "chan"), None, None, None, None),
        check_vma=False,
    )
```

time: 475 us -> 215 us (0.45)
  Pallas kernels: 449 us -> 215 us
  other arithmetic: 24.6 us -> 0 us
    pallas_call x1, Pallas kernels: 258 us -> 20.8 us  [on_device(): pl.pallas_call(finish_kernel, out_shape=jax.ShapeDtypeStruct((2, nblk, 2,...]
    transpose x1 -> x0, other arithmetic: 16.1 us -> none  [on_device(): turned = jnp.swapaxes(scaled, 0, 1)]
    reduce_sum x1 -> x0, other arithmetic: 7.83 us -> none  [on_device(): power = jnp.sum(wide * wide, axis=(1, 2))]
where the time goes in v2:
time: 215 us
  Pallas kernels  215 us (100%)
    pallas_call x1, Pallas kernels, on_device(): pl.pallas_call(functools.partial(turn_kernel, n, float(chans * NT)), out_...  194 us
    pallas_call x1, Pallas kernels, on_device(): pl.pallas_call(finish_kernel, out_shape=jax.ShapeDtypeStruct((2, nblk, 2,...  20.8 us

profile of v2, /device:TPU:13, one launch (start us, length us, event | category | flops | bytes accessed | tf_op | source)
XLA Modules:
  0.0 215.1 jit_solution(16011754947117782941)
XLA Ops:
  0.0 194.3 %turn.1 = (bf16[16,256,512]{2,1,0:T(8,128)(2,1)}, bf16[128,2,128,128]{3,2,1,0:T(8,128)(2,1)}, f32[32,128,128]{2,1,0:T(8,128)}, f32[32,8,128]{2,1,0:T(8,128)}) custom-call(bf16[256,32,512]{2,1,0:T(8,128)(2,1)} %x_ref.1, s32[32]{0:T(128)} %exps_ref.1, s32[2,128]{1,0:T(2,128)} %bitcast.3), custom_call_target="tpu_custom_call" | custom-call | tf_op jit(solution)/shard_map/turn/pallas_call | solution.py:216
  194.3 20.8 %finish.1 = bf16[2,128,2,128,128]{4,3,2,1,0:T(8,128)(2,1)} custom-call(bf16[32,128,512]{2,1,0:T(8,128)(2,1)} %bitcast.2, bf16[128,2,128,128]{3,2,1,0:T(8,128)(2,1)} %get-tuple-element.10.vis_ref, f32[32,128,128]{2,1,0:T(8,128)} %get-tuple-element.11.col_ref, f32[32,8,128]{2,1,0:T(8,128)} %get-tuple-element.12.rows, s32[2,128]{1,0:T(2,128)} %bitcast.4), custom_call_target="tpu_custom_call" | custom-call | tf_op jit(solution)/shard_map/finish/pallas_call | solution.py:245

commit v3 on v2

--- a/solution.py
+++ b/solution.py
@@ -23,7 +23,7 @@
     return (raw[:, :PANEL] * scale).astype(jnp.bfloat16), (raw[:, PANEL:] * scale).astype(jnp.bfloat16)
 
 
-def turn_kernel(n, total, x_ref, exps_ref, pairs_ref, late_ref, vis_ref, col_ref, row_ref,
+def turn_kernel(n, total, x_ref, exps_ref, pairs_ref, late_ref, vis_ref, row_ref,
                 raw, wide, outbox, early, stage, sums, ownpow, allpow, cols, rows,
                 send, recv, lsend, lrecv, psend, precv, insem, local):
     me = lax.axis_index("chan")
@@ -125,9 +125,7 @@
             rows[p] = jnp.broadcast_to(lax.rsqrt(mean), (8, PANEL))
             cols[p] = jnp.broadcast_to(lax.rsqrt(NT * mean), (PANEL, PANEL)).T
 
-    col_out = pltpu.make_async_copy(cols, col_ref, local.at[3])
-    row_out = pltpu.make_async_copy(rows, row_ref, local.at[4])
-    col_out.start()
+    row_out = pltpu.make_async_copy(rows, row_ref, local.at[3])
     row_out.start()
     own_early.wait()
 
@@ -145,7 +143,7 @@
         stage[k, 0] = re
         stage[k, 1] = im
 
-    vis_out = pltpu.make_async_copy(stage, vis_ref, local.at[5])
+    vis_out = pltpu.make_async_copy(stage, vis_ref, local.at[4])
     vis_out.start()
     own_late.wait()
 
@@ -154,18 +152,20 @@
         late_copy(off).wait()
 
     vis_out.wait()
-    col_out.wait()
     row_out.wait()
 
 
-def finish_kernel(data_ref, vis_ref, col_ref, rows, pairs_ref, out_ref, data, cols, first, stage, insem, sems):
+def finish_kernel(data_ref, vis_ref, rows, pairs_ref, out_ref, data, twist, cols, first, stage, insem, sems):
     nblk = pairs_ref.shape[1]
+    panels, _, width = data_ref.shape
+    half = width // 2
     groups = nblk // GROUP
-
-    data_in = pltpu.make_async_copy(data_ref, data, insem.at[groups])
-    cols_in = pltpu.make_async_copy(col_ref, cols, insem.at[groups + 1])
-    data_in.start()
-    cols_in.start()
+    loads = insem.shape[0] - groups
+    some = panels // loads
+
+    def load(j):
+        part = pl.ds(j * some, some)
+        return pltpu.make_async_copy(data_ref.at[part], data.at[part], insem.at[groups + j])
 
     def fetch(g):
         part = pl.ds(g * GROUP, GROUP)
@@ -179,21 +179,38 @@
         part = pl.ds(g * GROUP, GROUP)
         return pltpu.make_async_copy(stage.at[part], out_ref.at[1, part], sems.at[1, g])
 
+    for j in range(loads):
+        load(j).start()
     for g in range(groups):
         fetch(g).start()
-    data_in.wait()
-    cols_in.wait()
+
+    table = jnp.concatenate([rows[p, 0:1, :] for p in range(panels)]
+                            + [jnp.zeros((PANEL - panels, PANEL), jnp.float32)], axis=0).T * NT ** -0.5
+    for p in range(panels):
+        cols[p] = jnp.broadcast_to(table[:, p:p + 1], (PANEL, PANEL))
+
+    for j in range(loads):
+        load(j).wait()
+
+        @pl.loop(j * some, (j + 1) * some, unroll=2)
+        def _(p):
+            t = data[p].T
+            twist[p, :, :PANEL] = t
+            twist[p, :half, PANEL:] = -t[half:]
+            twist[p, half:, PANEL:] = t[:half]
 
     for g in range(groups):
-        @pl.loop(g * GROUP, (g + 1) * GROUP, unroll=4)
+        fetch(g).wait()
+        old(g).start()
+
+        @pl.loop(g * GROUP, (g + 1) * GROUP, unroll=GROUP)
         def _(k):
             p, q = pairs_ref[0, k], pairs_ref[1, k]
-            re, im = block_product(data[p], data[q], cols[p], rows[q, 0:1, :])
-            stage[k, 0] = re
-            stage[k, 1] = im
+            raw = jnp.dot(data[p], twist[q], preferred_element_type=jnp.float32)
+            scale = cols[p] * rows[q, 0:1, :]
+            stage[k, 0] = (raw[:, :PANEL] * scale).astype(jnp.bfloat16)
+            stage[k, 1] = (raw[:, PANEL:] * scale).astype(jnp.bfloat16)
         new(g).start()
-        fetch(g).wait()
-        old(g).start()
 
     for g in range(groups):
         old(g).wait()
@@ -205,7 +222,7 @@
     assert chans == 2 * n and ants % PANEL == 0
     nblk = pairs.shape[0]
     panels = n * ants // PANEL
-    size = 64
+    size = 32
     pieces = ants // size
     pairs = pairs.T
 
@@ -213,16 +230,15 @@
     vmem = pl.BlockSpec(memory_space=pltpu.VMEM)
     smem = pl.BlockSpec(memory_space=pltpu.SMEM)
     dma = pltpu.SemaphoreType.DMA
-    late, vis, cols, rows = pl.pallas_call(
+    late, vis, rows = pl.pallas_call(
         functools.partial(turn_kernel, n, float(chans * NT)),
         out_shape=[
             jax.ShapeDtypeStruct((n, ants, width), jnp.bfloat16),
             jax.ShapeDtypeStruct((nblk, 2, PANEL, PANEL), jnp.bfloat16),
-            jax.ShapeDtypeStruct((panels, PANEL, PANEL), jnp.float32),
             jax.ShapeDtypeStruct((panels, 8, PANEL), jnp.float32),
         ],
         in_specs=[hbm, smem, smem],
-        out_specs=[hbm, hbm, hbm, hbm],
+        out_specs=[hbm, hbm, hbm],
         scratch_shapes=[
             pltpu.VMEM((pieces, size, chans, width), jnp.bfloat16),
             pltpu.VMEM((width // 128, size * chans, 128), jnp.float32),
@@ -235,7 +251,7 @@
             pltpu.VMEM((panels, PANEL, PANEL), jnp.float32),
             pltpu.VMEM((panels, 8, PANEL), jnp.float32),
             dma((pieces, n)), dma((pieces, n)), dma((n,)), dma((n,)), dma((n,)), dma((n,)),
-            dma((pieces,)), dma((6,)),
+            dma((pieces,)), dma((5,)),
         ],
         compiler_params=pltpu.CompilerParams(
             collective_id=0, has_side_effects=True, vmem_limit_bytes=VMEM_LIMIT),
@@ -245,19 +261,20 @@
     return pl.pallas_call(
         finish_kernel,
         out_shape=jax.ShapeDtypeStruct((2, nblk, 2, PANEL, PANEL), jnp.bfloat16),
-        in_specs=[hbm, hbm, hbm, vmem, smem],
+        in_specs=[hbm, hbm, vmem, smem],
         out_specs=hbm,
         scratch_shapes=[
             pltpu.VMEM((panels, PANEL, width), jnp.bfloat16),
+            pltpu.VMEM((panels, width, 2 * PANEL), jnp.bfloat16),
             pltpu.VMEM((panels, PANEL, PANEL), jnp.float32),
             pltpu.VMEM((nblk, 2, PANEL, PANEL), jnp.bfloat16),
             pltpu.VMEM((nblk, 2, PANEL, PANEL), jnp.bfloat16),
-            dma((nblk // GROUP + 2,)),
+            dma((nblk // GROUP + 4,)),
             dma((2, nblk // GROUP)),
         ],
         compiler_params=pltpu.CompilerParams(vmem_limit_bytes=VMEM_LIMIT),
         name="finish",
-    )(late.reshape(panels, PANEL, width), vis, cols, rows, pairs)
+    )(late.reshape(panels, PANEL, width), vis, rows, pairs)
 
 
 def solution(mesh):

time: 215 us -> 204 us (0.949)
  Pallas kernels: 215 us -> 204 us
    pallas_call x1, Pallas kernels: 20.8 us -> 11.3 us  [on_device(): pl.pallas_call(finish_kernel, out_shape=jax.ShapeDtypeStruct((2, nblk, 2,...]
where the time goes in v3:
time: 204 us
  Pallas kernels  204 us (100%)
    pallas_call x1, Pallas kernels, on_device(): pl.pallas_call(functools.partial(turn_kernel, n, float(chans * NT)), out_...  193 us
    pallas_call x1, Pallas kernels, on_device(): pl.pallas_call(finish_kernel, out_shape=jax.ShapeDtypeStruct((2, nblk, 2,...  11.3 us

profile of v3, /device:TPU:13, one launch (start us, length us, event | category | flops | bytes accessed | tf_op | source)
XLA Modules:
  0.0 203.9 jit_solution(10279422776220987237)
XLA Ops:
  0.0 192.6 %turn.1 = (bf16[16,256,512]{2,1,0:T(8,128)(2,1)}, bf16[128,2,128,128]{3,2,1,0:T(8,128)(2,1)}, f32[32,8,128]{2,1,0:T(8,128)}) custom-call(bf16[256,32,512]{2,1,0:T(8,128)(2,1)} %x_ref.1, s32[32]{0:T(128)} %exps_ref.1, s32[2,128]{1,0:T(2,128)} %bitcast.3), custom_call_target="tpu_custom_call" | custom-call | tf_op jit(solution)/shard_map/turn/pallas_call | solution.py:233
  192.6 11.3 %finish.1 = bf16[2,128,2,128,128]{4,3,2,1,0:T(8,128)(2,1)} custom-call(bf16[32,128,512]{2,1,0:T(8,128)(2,1)} %bitcast.2, bf16[128,2,128,128]{3,2,1,0:T(8,128)(2,1)} %get-tuple-element.9.vis_ref, f32[32,8,128]{2,1,0:T(8,128)} %get-tuple-element.10.rows, s32[2,128]{1,0:T(2,128)} %bitcast.4), custom_call_target="tpu_custom_call" | custom-call | tf_op jit(solution)/shard_map/finish/pallas_call | solution.py:261
